TPU v7x, 768 devices: a whole 4x8x12 slice. The times are simulated.
768 devices in a mesh: tensor: 8 (over x, y_hi), dp: 96 (over y_lo, z, core).
Axes of the slice: x: 4, y: 8 (y_hi: 2, y_lo: 4; y = y_hi * 4 + y_lo), z: 12, core: 2. Of those that a mesh axis runs over, the one named last changes fastest.
Arguments:
- gate: bfloat16 [192, 36864], P('dp', 'tensor'), may hold values from -6 to 6
- up: bfloat16 [192, 36864], P('dp', 'tensor'), may hold values from -6 to 6
- down_weight: bfloat16 [36864, 18432], P('tensor', 'dp'), may hold values from -0.03125 to 0.03125
- out_grad: bfloat16 [192, 18432], P('tensor', 'dp'), may hold values from -20 to 20
Outputs:
- output: bfloat16 [192, 18432], P('tensor', 'dp')
- grad_down: bfloat16 [36864, 18432], P('tensor', 'dp')
- grad_gate: bfloat16 [192, 36864], P('dp', 'tensor')
- grad_up: bfloat16 [192, 36864], P('dp', 'tensor')
All inputs are finite; a program needn't handle non-finite values.
Results may differ from a plain program's by a relative error of at most 0.0049.
Values may be sent and summed in bfloat16 or wider, within the bound.
No kernel may reach another device: no remote copies, remote signals or barrier semaphores. Data moves between devices by JAX's collectives and lax.ppermute only.
A program may use at most 32 MiB of HBM per device.

v0:
```python
import jax
import jax.numpy as jnp
from jax import lax
from jax.sharding import PartitionSpec as P


def local(gate, up, down_weight, out_grad):
    gate32 = gate.astype(jnp.float32)
    up32 = up.astype(jnp.float32)
    sigmoid = jax.nn.sigmoid(gate32)
    silu = gate32 * sigmoid
    hidden = (silu * up32).astype(jnp.bfloat16)
    gathered = lax.all_gather(hidden, "dp", axis=0, tiled=True)
    partial_out = jnp.dot(gathered, down_weight, preferred_element_type=jnp.float32)
    output = lax.psum_scatter(partial_out, "tensor", scatter_dimension=0, tiled=True).astype(
        jnp.bfloat16
    )
    grad_all = lax.all_gather(out_grad, "tensor", axis=0, tiled=True)
    hidden_grad = lax.psum_scatter(
        lax.dot_general(
            grad_all, down_weight, (((1,), (1,)), ((), ())), preferred_element_type=jnp.float32
        ),
        "dp",
        scatter_dimension=0,
        tiled=True,
    )
    weight_sum = lax.dot_general(
        gathered, grad_all, (((0,), (0,)), ((), ())), preferred_element_type=jnp.float32
    )
    grad_down = weight_sum.astype(jnp.bfloat16)
    grad_gate = (hidden_grad * up32 * sigmoid * (1.0 + gate32 * (1.0 - sigmoid))).astype(
        jnp.bfloat16
    )
    grad_up = (hidden_grad * silu).astype(jnp.bfloat16)
    return (output, grad_down, grad_gate, grad_up)


def solution(mesh):
    placed = (P("dp", "tensor"), P("dp", "tensor"), P("tensor", "dp"), P("tensor", "dp"))
    return jax.shard_map(
        local,
        mesh=mesh,
        in_specs=placed,
        out_specs=(P("tensor", "dp"), P("tensor", "dp"), P("dp", "tensor"), P("dp", "tensor")),
        check_vma=False,
    )
```

profile of v0, /device:TPU:6, one launch (start us, length us, event | category | flops | bytes accessed | tf_op | source)
XLA Modules:
  0.0 1129.8 jit_solution(263656444511931746)
XLA Ops:
  7.2 0.0 copy-start
  7.2 0.0 all-reduce.3.cloned.1.call-start
  7.2 51.0 %all_gather.7 = bf16[192,192]{1,0:T(8,128)(2,1)S(1)} all-gather(bf16[24,192]{1,0:T(8,128)(2,1)} %param.7), channel_id=1, replica_groups=mesh['tensor'=8,'dp'=96] {'tensor'}, dimensions={0}, use_global_device_ids=true | all-gather | bytes 82944 | tf_op jit(solution)/shard_map/all_gather | solution.py:18
  58.2 0.0 copy-start.1
  58.2 0.6 copy-done.1
  58.9 0.0 copy-done
  58.9 2.4 fusion.11
  61.3 0.0 copy-start.2
  61.3 0.0 copy-start.3
  61.3 0.0 all-reduce.3.cloned.1.call-update
  61.3 0.0 all-gather.3.cloned.1.call-start
  61.4 1.3 dynamic-slice
  63.3 796.6 %all-reduce.3.cloned.1.call-done = f32[192,4608]{1,0:T(8,128)} async-done(((f32[192,4608]{1,0:T(8,128)}), f32[192,4608]{1,0:T(8,128)}) %all-reduce.3.cloned.1.call-update) | async-done | bytes 3538960
  859.9 0.0 copy-done.2
  859.9 1.6 multiply_convert_fusion
  861.5 0.0 copy-done.3
  861.5 1.6 fusion.3
  863.1 0.0 all-gather.3.cloned.1.call-update
  863.1 0.0 reduce-scatter.2.cloned.1.call-start
  863.2 162.0 %all-gather.3.cloned.1.call-done = bf16[96,2,4608]{2,1,0:T(2,128)(2,1)} async-done(((bf16[1,2,4608]{2,1,0:T(2,128)(2,1)}), bf16[96,2,4608]{2,1,0:T(2,128)(2,1)}) %all-gather.3.cloned.1.call-update) | async-done | bytes 1769488 | tf_op jit(solution)/shard_map/all_gather | solution.py:13
  1025.2 2.6 reshape.9
  1027.8 1.3 fusion.10
  1029.1 0.0 reduce-scatter.2.cloned.1.call-update
  1029.1 2.8 convolution_convert_fusion
  1031.9 90.1 %reduce-scatter.2.cloned.1.call-done = f32[24,192]{1,0:T(8,128)} async-done(((f32[192,192]{1,0:T(8,128)}), f32[24,192]{1,0:T(8,128)}) %reduce-scatter.2.cloned.1.call-update) | async-done | bytes 18448 | tf_op jit(solution)/shard_map/reduce_scatter | solution.py:15
  1122.0 1.3 convert_element_type.24
Async XLA Ops:
  7.2 51.7 %copy-start = (bf16[4608,192]{0,1:T(8,128)(2,1)S(1)}, bf16[4608,192]{0,1:T(8,128)(2,1)}, u32[]{:S(2)}) copy-start(bf16[4608,192]{0,1:T(8,128)(2,1)} %param.6) | copy-start | bytes 5308420
  7.2 852.7 %all-reduce.3.cloned.1.call-start = ((), (), s32[]{:S(2)}) async-start(), calls=%async_computation.3 | async-start | bytes 7077888
  58.2 0.6 copy-start.1
  61.3 798.6 %copy-start.2 = (bf16[2,4608]{1,0:T(2,128)(2,1)S(1)}, bf16[2,4608]{1,0:T(2,128)(2,1)}, u32[]{:S(2)}) copy-start(bf16[2,4608]{1,0:T(2,128)(2,1)} %param.4) | copy-start | bytes 55300
  61.3 800.2 %copy-start.3 = (bf16[2,4608]{1,0:T(2,128)(2,1)S(1)}, bf16[2,4608]{1,0:T(2,128)(2,1)}, u32[]{:S(2)}) copy-start(bf16[2,4608]{1,0:T(2,128)(2,1)} %param.5) | copy-start | bytes 55300
  61.3 963.9 %all-gather.3.cloned.1.call-start = ((), (), s32[]{:S(2)}) async-start(), calls=%async_computation.2 | async-start | bytes 1787904 | tf_op jit(solution)/shard_map/all_gather | solution.py:13
  863.1 258.9 %reduce-scatter.2.cloned.1.call-start = ((), (), s32[]{:S(2)}) async-start(), calls=%async_computation.1 | async-start | bytes 221184 | tf_op jit(solution)/shard_map/reduce_scatter | solution.py:15
Sparse Core Ops, SparseCore 0:
  61.4 798.4 all-reduce.2
  863.3 161.8 all-gather.2
  1031.0 90.9 reduce-scatter.1
where the time goes:
time: 1130 us
  waiting for transfers between devices  1050 us (93%)
  blocking collectives  51 us (5%)
  between operations  14.4 us (1%)
    unnamed x4, waiting for transfers between devices  797 us
    all_gather x1, waiting for transfers between devices, local(): gathered = lax.all_gather(hidden, 'dp', axis=0, tiled=True)  162 us
    reduce_scatter x1, waiting for transfers between devices, local(): lax.psum_scatter(partial_out, 'tensor', scatter_dimension=0, tiled=True)  90.1 us
    all_gather x1, blocking collectives, local(): grad_all = lax.all_gather(out_grad, 'tensor', axis=0, tiled=True)  51 us
  transfers between devices with their start and end apart: 3, of which 3 were waited for; matrix products, arithmetic and copies ran while one was open for 0% of the time, Pallas kernels for 0%

commit v1 on v0

v1 whole, which is shorter than its diff:
```python
import numpy as np

import jax
import jax.numpy as jnp
from jax import lax
from jax.sharding import PartitionSpec as P

YL, Z, C = 4, 12, 2
NEAR = 4
FAR = Z // NEAR


def dp_index(yl, z, c):
    return (yl * Z + z) * C + c


WIDE = [[dp_index(y, z, 0) for z in range(Z)] for y in range(YL)] + [
    [dp_index(y, n + NEAR * f, 1) for y in range(YL) for f in range(FAR)] for n in range(NEAR)
]
NARROW = [[dp_index(y, z, 0) for y in range(YL)] for z in range(Z)] + [
    [dp_index(y, n + NEAR * f, 1) for n in range(NEAR)] for y in range(YL) for f in range(FAR)
]
ORDER = [dp_index(y, z, 0) for y in range(YL) for z in range(Z)] + [
    dp_index(y, n + NEAR * f, 1) for n in range(NEAR) for y in range(YL) for f in range(FAR)
]
SWAP = [(i, i ^ 1) for i in range(YL * Z * C)]
f32, bf16 = jnp.float32, jnp.bfloat16


def row_order(each):
    return np.array([[i * each + r for r in range(each)] for i in ORDER], np.int32).reshape(-1)


def exchange(blocks, groups):
    return lax.all_to_all(blocks, "dp", 0, 0, axis_index_groups=groups)


def total(blocks):
    parts = [blocks[i].astype(f32) for i in range(blocks.shape[0])]
    while len(parts) > 1:
        parts = [a + b for a, b in zip(parts[::2], parts[1::2])] + parts[len(parts) // 2 * 2 :]
    return parts[0]


def dot(a, b, ca, cb):
    return lax.dot_general(a, b, (((ca,), (cb,)), ((), ())), preferred_element_type=f32)


def tie(*arrays):
    return lax.optimization_barrier(arrays)

BACK = [group[::-1] for group in WIDE]


def partner(mask, members):
    return [(i, i ^ mask) for i in range(members)]


def gather_tokens(rows):
    for mask in (1, 2, 4):
        rows = jnp.concatenate([rows, lax.ppermute(rows, "tensor", partner(mask, 8))], axis=0)
    return rows


def scatter_tokens(rows):
    for mask in (4, 2, 1):
        half = rows.shape[0] // 2
        theirs = lax.ppermute(rows[half:].astype(bf16), "tensor", partner(mask, 8))
        rows = rows[:half].astype(f32) + theirs.astype(f32)
    return rows


def placement(each, tokens):
    core = lax.axis_index("dp") % C
    mine = lax.axis_index("tensor")
    rows = row_order(each)
    token_at = jnp.where(core == 0, rows, np.roll(rows, tokens // 2))
    column = jnp.arange(tokens, dtype=jnp.int32)
    own = tokens // 8
    token_of = jnp.bitwise_xor(mine, column // own) * own + column % own
    return (token_at[:, None] == token_of[None, :]).astype(bf16)


def local(gate, up, down_weight, out_grad):
    each, units = gate.shape
    own, width = out_grad.shape
    tokens = own * 8
    half = tokens // 2
    few = half // 4
    place = placement(each, tokens)

    gate32 = gate.astype(f32)
    up32 = up.astype(f32)
    sigmoid = jax.nn.sigmoid(gate32)
    silu = gate32 * sigmoid
    hidden = (silu * up32).astype(bf16)

    h1 = exchange(jnp.broadcast_to(hidden[None], (12, each, units)), WIDE).reshape(few, units)

    grads = dot(place, gather_tokens(out_grad), 1, 0).astype(bf16)
    received = lax.ppermute(dot(grads[half:], down_weight, 1, 1).astype(bf16), "dp", SWAP)
    r1 = (dot(grads[:half], down_weight, 1, 1) + received.astype(f32)).astype(bf16)

    h2 = exchange(jnp.broadcast_to(h1[None], (4, few, units)), NARROW).reshape(half, units)
    h2, r1 = tie(h2, r1)
    r2 = total(exchange(r1.reshape(4, few, units), NARROW)).astype(bf16).reshape(12, each, units)
    r3 = exchange(r2[::-1], BACK)
    other = lax.ppermute(h2, "dp", SWAP)
    partial_out = jnp.concatenate(
        [dot(h2, down_weight, 1, 0).astype(bf16), dot(other, down_weight, 1, 0).astype(bf16)], axis=0
    )
    output = scatter_tokens(dot(place, partial_out, 0, 0)).astype(bf16)

    hidden_grad = total(r3)
    grad_down = dot(jnp.concatenate([h2, other], axis=0), grads, 0, 0).astype(bf16)
    grad_gate = (hidden_grad * up32 * sigmoid * (1.0 + gate32 * (1.0 - sigmoid))).astype(bf16)
    grad_up = (hidden_grad * silu).astype(bf16)
    return (output, grad_down, grad_gate, grad_up)


def solution(mesh):
    placed = (P("dp", "tensor"), P("dp", "tensor"), P("tensor", "dp"), P("tensor", "dp"))
    return jax.shard_map(
        local,
        mesh=mesh,
        in_specs=placed,
        out_specs=(P("tensor", "dp"), P("tensor", "dp"), P("dp", "tensor"), P("dp", "tensor")),
        check_vma=False,
    )
```

time: 1130 us -> 102 us (0.09)
  waiting for transfers between devices: 1050 us -> 19.5 us
  starting transfers between devices: 0.12 us -> 63.7 us
  blocking collectives: 51 us -> 0 us
  between operations: 14.4 us -> 0.92 us
    unnamed x4 -> x0, waiting for transfers between devices: 797 us -> none
    all_gather x1 -> x0, waiting for transfers between devices: 162 us -> none  [local(): gathered = lax.all_gather(hidden, 'dp', axis=0, tiled=True)]
    reduce_scatter x1 -> x0, waiting for transfers between devices: 90.1 us -> none  [local(): lax.psum_scatter(partial_out, 'tensor', scatter_dimension=0, tiled=True)]
    all_gather x1 -> x0, blocking collectives: 51 us -> none  [local(): grad_all = lax.all_gather(out_grad, 'tensor', axis=0, tiled=True)]
    all_to_all x0 -> x4, starting transfers between devices: none -> 33.3 us  [exchange(): return lax.all_to_all(blocks, 'dp', 0, 0, axis_index_groups=groups)]
    ppermute x0 -> x8, starting transfers between devices: none -> 30.4 us  [the longest x3 13.9 us: gather_tokens(): lax.ppermute(rows, 'tensor', partner(mask, 8))]
    ppermute x0 -> x8, waiting for transfers between devices: none -> 14.4 us  [the longest x3 6.1 us: gather_tokens(): lax.ppermute(rows, 'tensor', partner(mask, 8))]
  transfers between devices with their start and end apart: 3 -> 12, of which waited for: 3 -> 8; matrix products, arithmetic and copies ran while one was open for 0% -> 13% of each run, Pallas kernels for 0% -> 0%
where the time goes in v1:
time: 102 us; the launch traced here: 101 us
  starting transfers between devices  63.7 us (62%)
  waiting for transfers between devices  19.5 us (19%)
  matrix products  6.71 us (7%)
  other arithmetic  5.89 us (6%)
  local copies, waits for them, and re-layouts  4.43 us (4%)
    all_to_all x4, starting transfers between devices, exchange(): return lax.all_to_all(blocks, 'dp', 0, 0, axis_index_groups=groups)  33.3 us
    ppermute x3, starting transfers between devices, gather_tokens(): lax.ppermute(rows, 'tensor', partner(mask, 8))  13.9 us
    ppermute x3, starting transfers between devices, scatter_tokens(): theirs = lax.ppermute(rows[half:].astype(bf16), 'tensor', partner(mask, 8))  12.7 us
    dot_general x7, matrix products, dot(): lax.dot_general(a, b, (((ca,), (cb,)), ((), ())), preferred_element_type=...  6.71 us
    ppermute x3, waiting for transfers between devices, gather_tokens(): lax.ppermute(rows, 'tensor', partner(mask, 8))  6.1 us
    all_to_all x4, waiting for transfers between devices, exchange(): return lax.all_to_all(blocks, 'dp', 0, 0, axis_index_groups=groups)  5.11 us
    ppermute x3, waiting for transfers between devices, scatter_tokens(): theirs = lax.ppermute(rows[half:].astype(bf16), 'tensor', partner(mask, 8))  4.17 us
    ppermute x1, waiting for transfers between devices, local(): lax.ppermute(dot(grads[half:], down_weight, 1, 1).astype(bf16), 'dp', SWAP)  2.39 us
  transfers between devices with their start and end apart: 12, of which 8 were waited for; matrix products, arithmetic and copies ran while one was open for 13% of the time, Pallas kernels for 0%

profile of v1, /device:TPU:6, one launch (start us, length us, event | category | flops | bytes accessed | tf_op | source)
XLA Modules:
  0.0 101.1 jit_solution(12646856655874678403)
XLA Ops:
  0.6 0.0 copy-start
  0.6 1.5 %fusion.25 = (bf16[2,4608]{1,0:T(2,128)(2,1)S(1)}, f32[2,4608]{1,0:T(2,128)}) fusion(bf16[2,4608]{1,0:T(2,128)(2,1)} %param.7, bf16[2,4608]{1,0:T(2,128)(2,1)} %param.6), kind=kLoop, calls=%fused_computation.40 | loop fusion | flops 73728 | bytes 92160 | tf_op jit(solution)/shard_map/convert_element_type | solution.py:96
  2.2 0.8 broadcast_in_dim.6
  3.0 15.2 %all-to-all-start = ((bf16[12,2,4608]{2,1,0:T(2,128)(2,1)}), bf16[12,2,4608]{2,1,0:T(2,128)(2,1)S(1)}, u32[]{:S(2)}, u32[]{:S(2)}) async-start(bf16[12,2,4608]{2,1,0:T(2,128)(2,1)} %broadcast_in_dim.6), calls=%async_computation | async-start | bytes 442368 | tf_op jit(solution)/shard_map/all_to_all | solution.py:35
  18.1 0.0 copy-start.7
  18.2 0.0 copy-start.8
  18.2 0.0 copy-start.9
  18.2 7.9 %collective-permute-start = (bf16[24,192]{1,0:T(8,128)(2,1)}, bf16[24,192]{1,0:T(8,128)(2,1)S(1)}, u32[]{:S(2)}, u32[]{:S(2)}) collective-permute-start(bf16[24,192]{1,0:T(8,128)(2,1)} %param.9), channel_id=1, source_target_pairs={{0,96},{96,0},{192,288},{288,192},{384,480},{480,384},{576,672},{6... | collective-permute-start | bytes 27656 | tf_op jit(solution)/shard_map/ppermute | solution.py:61
  26.1 2.0 %collective-permute-done = bf16[24,192]{1,0:T(8,128)(2,1)S(1)} collective-permute-done((bf16[24,192]{1,0:T(8,128)(2,1)}, bf16[24,192]{1,0:T(8,128)(2,1)S(1)}, u32[]{:S(2)}, u32[]{:S(2)}) %collective-permute-start) | collective-permute-done | bytes 9248 | tf_op jit(solution)/shard_map/ppermute | solution.py:61
  28.0 0.7 pad_maximum_fusion.1
  28.7 2.7 %collective-permute-start.1 = (bf16[48,192]{1,0:T(8,128)(2,1)S(1)}, bf16[48,192]{1,0:T(8,128)(2,1)S(1)}, u32[]{:S(2)}, u32[]{:S(2)}) collective-permute-start(bf16[48,192]{1,0:T(8,128)(2,1)S(1)} %pad_maximum_fusion.1), channel_id=1, source_target_pairs={{0,192},{96,288},{192,0},{288,96},{384,576},{480,672},{576,384},{6... | collective-permute-start | bytes 55304 | tf_op jit(solution)/shard_map/ppermute | solution.py:61
  31.5 2.7 %all-to-all-done = bf16[12,2,4608]{2,1,0:T(2,128)(2,1)S(1)} async-done(((bf16[12,2,4608]{2,1,0:T(2,128)(2,1)}), bf16[12,2,4608]{2,1,0:T(2,128)(2,1)S(1)}, u32[]{:S(2)}, u32[]{:S(2)}) %all-to-all-start) | async-done | bytes 221216 | tf_op jit(solution)/shard_map/all_to_all | solution.py:35
  34.2 0.1 broadcast_in_dim.7
  34.3 1.0 broadcast_in_dim.8
  35.2 5.0 %all-to-all-start.1 = ((bf16[4,24,4608]{2,1,0:T(8,128)(2,1)}), bf16[4,24,4608]{2,1,0:T(8,128)(2,1)S(1)}, u32[]{:S(2)}, u32[]{:S(2)}) async-start(bf16[4,24,4608]{2,1,0:T(8,128)(2,1)} %broadcast_in_dim.8), calls=%async_computation.1 | async-start | bytes 1769472 | tf_op jit(solution)/shard_map/all_to_all | solution.py:35
  40.2 0.0 collective-permute-done.1
  40.2 0.0 copy-done.7
  40.3 3.3 %collective-permute-start.2 = (bf16[96,192]{1,0:T(8,128)(2,1)S(1)}, bf16[96,192]{1,0:T(8,128)(2,1)S(1)}, u32[]{:S(2)}, u32[]{:S(2)}) collective-permute-start(bf16[96,192]{1,0:T(8,128)(2,1)S(1)} %pad_maximum_fusion), channel_id=1, source_target_pairs={{0,384},{96,480},{192,576},{288,672},{384,0},{480,96},{576,192},{6... | collective-permute-start | bytes 110600 | tf_op jit(solution)/shard_map/ppermute | solution.py:61
  43.6 0.0 copy-done.8
  43.6 0.0 copy-done.9
  43.6 4.1 %collective-permute-done.2 = bf16[96,192]{1,0:T(8,128)(2,1)S(1)} collective-permute-done((bf16[96,192]{1,0:T(8,128)(2,1)S(1)}, bf16[96,192]{1,0:T(8,128)(2,1)S(1)}, u32[]{:S(2)}, u32[]{:S(2)}) %collective-permute-start.2) | collective-permute-done | bytes 36896 | tf_op jit(solution)/shard_map/ppermute | solution.py:61
  47.8 0.2 convolution_convert_fusion.2
  48.0 0.0 copy-done
  48.0 0.0 copy-start.5
  48.0 0.4 convolution_convert_fusion.1
  48.4 1.9 %collective-permute-start.3 = (bf16[96,4608]{1,0:T(8,128)(2,1)S(1)}, bf16[96,4608]{1,0:T(8,128)(2,1)S(1)}, u32[]{:S(2)}, u32[]{:S(2)}) collective-permute-start(bf16[96,4608]{1,0:T(8,128)(2,1)S(1)} %convolution_convert_fusion.1), channel_id=1, source_target_pairs={{0,1},{1,0},{2,3},{3,2},{4,5},{5,4},{6,7},{7,6},{8,9},{9,8},{10,11... | collective-permute-start | bytes 2654216 | tf_op jit(solution)/shard_map/ppermute | solution.py:101
  50.3 2.4 %collective-permute-done.3 = bf16[96,4608]{1,0:T(8,128)(2,1)S(1)} collective-permute-done((bf16[96,4608]{1,0:T(8,128)(2,1)S(1)}, bf16[96,4608]{1,0:T(8,128)(2,1)S(1)}, u32[]{:S(2)}, u32[]{:S(2)}) %collective-permute-start.3) | collective-permute-done | bytes 884768 | tf_op jit(solution)/shard_map/ppermute | solution.py:101
  52.7 0.0 copy-done.5
  52.7 1.4 %add_convert_fusion = bf16[96,4608]{1,0:T(8,128)(2,1)} fusion(bf16[96,4608]{1,0:T(8,128)(2,1)S(1)} %collective-permute-done.3, bf16[4608,192]{0,1:T(8,128)(2,1)S(1)} %copy-done, bf16[192,192]{1,0:T(8,128)(2,1)S(1)} %convolution_convert_fusion.2), kind=kOutput, calls=%fused_computation.5 | convolution fusion | flops 171196416 | bytes 3588096 | tf_op jit(solution)/shard_map/dot_general | solution.py:46
  54.1 0.3 all-to-all-done.1
  54.4 4.8 %all-to-all-start.2 = ((bf16[4,24,4608]{2,1,0:T(8,128)(2,1)}), bf16[4,24,4608]{2,1,0:T(8,128)(2,1)S(1)}, u32[]{:S(2)}, u32[]{:S(2)}) async-start(bf16[4,24,4608]{2,1,0:T(8,128)(2,1)} %bitcast.1), calls=%async_computation.2 | async-start | bytes 1769472 | tf_op jit(solution)/shard_map/all_to_all | solution.py:35
  59.2 1.9 %collective-permute-start.4 = (bf16[96,4608]{1,0:T(8,128)(2,1)S(1)}, bf16[96,4608]{1,0:T(8,128)(2,1)S(1)}, u32[]{:S(2)}, u32[]{:S(2)}) collective-permute-start(bf16[96,4608]{1,0:T(8,128)(2,1)S(1)} %bitcast.14), channel_id=1, source_target_pairs={{0,1},{1,0},{2,3},{3,2},{4,5},{5,4},{6,7},{7,6},{8,9},{9,8},{10,11... | collective-permute-start | bytes 2654216 | tf_op jit(solution)/shard_map/ppermute | solution.py:108
  61.1 0.7 convolution_convert_fusion.4
  61.8 1.7 %collective-permute-done.4 = bf16[96,4608]{1,0:T(8,128)(2,1)S(1)} collective-permute-done((bf16[96,4608]{1,0:T(8,128)(2,1)S(1)}, bf16[96,4608]{1,0:T(8,128)(2,1)S(1)}, u32[]{:S(2)}, u32[]{:S(2)}) %collective-permute-start.4) | collective-permute-done | bytes 884768 | tf_op jit(solution)/shard_map/ppermute | solution.py:108
  63.5 0.0 copy-start.1
  63.5 0.7 convolution_convert_fusion.3
  64.2 0.3 fusion.3
  64.5 3.3 %collective-permute-start.5 = (bf16[96,192]{1,0:T(8,128)(2,1)S(1)}, bf16[96,192]{1,0:T(8,128)(2,1)S(1)}, u32[]{:S(2)}, u32[]{:S(2)}) collective-permute-start(bf16[96,192]{1,0:T(8,128)(2,1)S(1)} %slice.153), channel_id=1, source_target_pairs={{0,384},{96,480},{192,576},{288,672},{384,0},{480,96},{576,192},{6... | collective-permute-start | bytes 110600 | tf_op jit(solution)/shard_map/ppermute | solution.py:68
  67.8 4.2 %collective-permute-done.5 = bf16[96,192]{1,0:T(8,128)(2,1)S(1)} collective-permute-done((bf16[96,192]{1,0:T(8,128)(2,1)S(1)}, bf16[96,192]{1,0:T(8,128)(2,1)S(1)}, u32[]{:S(2)}, u32[]{:S(2)}) %collective-permute-start.5) | collective-permute-done | bytes 36896 | tf_op jit(solution)/shard_map/ppermute | solution.py:68
  72.0 0.0 copy-start.3
  72.0 0.6 slice.154
  72.7 0.0 copy-done.1
  72.7 0.0 copy-done.3
  72.7 2.7 %collective-permute-start.6 = (bf16[48,192]{1,0:T(8,128)(2,1)}, bf16[48,192]{1,0:T(8,128)(2,1)}, u32[]{:S(2)}, u32[]{:S(2)}) collective-permute-start(bf16[48,192]{1,0:T(8,128)(2,1)} %slice.154), channel_id=1, source_target_pairs={{0,192},{96,288},{192,0},{288,96},{384,576},{480,672},{576,384},{6... | collective-permute-start | bytes 55304 | tf_op jit(solution)/shard_map/ppermute | solution.py:68
  75.4 0.0 all-to-all-done.2
  75.4 0.8 add_convert_fusion.1
  76.2 1.0 %convert_element_type.146 = bf16[12,2,4608]{2,1,0:T(2,128)(2,1)S(1)} reshape(bf16[1,24,4608]{2,1,0:T(8,128)(2,1)} %add_convert_fusion.1) | data formatting | bytes 442368 | tf_op jit(solution)/shard_map/convert_element_type | solution.py:106
  77.2 0.9 rev.3
  78.1 8.3 %all-to-all-start.3 = ((bf16[12,2,4608]{2,1,0:T(2,128)(2,1)}), bf16[12,2,4608]{2,1,0:T(2,128)(2,1)S(1)}, u32[]{:S(2)}, u32[]{:S(2)}) async-start(bf16[12,2,4608]{2,1,0:T(2,128)(2,1)} %rev.3), calls=%async_computation.3 | async-start | bytes 442368 | tf_op jit(solution)/shard_map/all_to_all | solution.py:35
  86.4 0.0 collective-permute-done.6
  86.4 0.8 slice_add_fusion.1
  87.2 0.0 copy-start.2
  87.2 0.0 copy-start.4
  87.2 0.0 copy-start.6
  87.3 6.6 %collective-permute-start.7 = (bf16[24,192]{1,0:T(8,128)(2,1)S(1)}, bf16[24,192]{1,0:T(8,128)(2,1)S(1)}, u32[]{:S(2)}, u32[]{:S(2)}) collective-permute-start(bf16[24,192]{1,0:T(8,128)(2,1)S(1)} %slice.155), channel_id=1, source_target_pairs={{0,96},{96,0},{192,288},{288,192},{384,480},{480,384},{576,672},{6... | collective-permute-start | bytes 27656 | tf_op jit(solution)/shard_map/ppermute | solution.py:68
  93.9 3.1 %convolution_convert_fusion = bf16[4608,192]{0,1:T(8,128)(2,1)} fusion(bf16[192,192]{1,0:T(8,128)(2,1)} %copy-done.5, bf16[96,4608]{1,0:T(8,128)(2,1)} %copy-done.1, bf16[96,4608]{1,0:T(8,128)(2,1)S(1)} %bitcast.16), kind=kOutput, calls=%fused_computation | convolution fusion | flops 344162304 | bytes 3612672 | tf_op jit(solution)/shard_map/dot_general | solution.py:46
  97.0 0.0 collective-permute-done.7
  97.0 0.6 fusion.34
  97.6 2.1 %all-to-all-done.3 = bf16[12,2,4608]{2,1,0:T(2,128)(2,1)S(1)} async-done(((bf16[12,2,4608]{2,1,0:T(2,128)(2,1)}), bf16[12,2,4608]{2,1,0:T(2,128)(2,1)S(1)}, u32[]{:S(2)}, u32[]{:S(2)}) %all-to-all-start.3) | async-done | bytes 221216 | tf_op jit(solution)/shard_map/all_to_all | solution.py:35
  99.7 0.0 copy-done.2
  99.7 0.0 copy-done.4
  99.7 0.7 fusion.33
  100.5 0.0 copy-done.6
  100.5 0.7 fusion.28
  (5 shorter events, 0.0 us)
Async XLA Ops:
  0.6 47.4 %copy-start = (bf16[4608,192]{0,1:T(8,128)(2,1)S(1)}, bf16[4608,192]{0,1:T(8,128)(2,1)}, u32[]{:S(2)}) copy-start(bf16[4608,192]{0,1:T(8,128)(2,1)} %param.8) | copy-start | bytes 5308420
  3.0 31.2 %all-to-all-start = ((bf16[12,2,4608]{2,1,0:T(2,128)(2,1)}), bf16[12,2,4608]{2,1,0:T(2,128)(2,1)S(1)}, u32[]{:S(2)}, u32[]{:S(2)}) async-start(bf16[12,2,4608]{2,1,0:T(2,128)(2,1)} %broadcast_in_dim.6), calls=%async_computation | async-start | bytes 442368 | tf_op jit(solution)/shard_map/all_to_all | solution.py:35
  18.1 22.1 %copy-start.7 = (bf16[24,192]{1,0:T(8,128)(2,1)S(1)}, bf16[24,192]{1,0:T(8,128)(2,1)}, u32[]{:S(2)}) copy-start(bf16[24,192]{1,0:T(8,128)(2,1)} %param.9) | copy-start | bytes 27652
  18.2 25.4 %copy-start.8 = (s32[192]{0:T(256)S(1)}, s32[192]{0:T(256)}, u32[]{:S(2)}) copy-start(s32[192]{0:T(256)} %constant.46.clone) | copy-start | bytes 2308
  18.2 25.4 %copy-start.9 = (s32[192]{0:T(256)S(1)}, s32[192]{0:T(256)}, u32[]{:S(2)}) copy-start(s32[192]{0:T(256)} %constant.45.clone) | copy-start | bytes 2308
  18.2 9.8 %collective-permute-start = (bf16[24,192]{1,0:T(8,128)(2,1)}, bf16[24,192]{1,0:T(8,128)(2,1)S(1)}, u32[]{:S(2)}, u32[]{:S(2)}) collective-permute-start(bf16[24,192]{1,0:T(8,128)(2,1)} %param.9), channel_id=1, source_target_pairs={{0,96},{96,0},{192,288},{288,192},{384,480},{480,384},{576,672},{6... | collective-permute-start | bytes 27656 | tf_op jit(solution)/shard_map/ppermute | solution.py:61
  28.7 11.5 %collective-permute-start.1 = (bf16[48,192]{1,0:T(8,128)(2,1)S(1)}, bf16[48,192]{1,0:T(8,128)(2,1)S(1)}, u32[]{:S(2)}, u32[]{:S(2)}) collective-permute-start(bf16[48,192]{1,0:T(8,128)(2,1)S(1)} %pad_maximum_fusion.1), channel_id=1, source_target_pairs={{0,192},{96,288},{192,0},{288,96},{384,576},{480,672},{576,384},{6... | collective-permute-start | bytes 55304 | tf_op jit(solution)/shard_map/ppermute | solution.py:61
  35.2 19.2 %all-to-all-start.1 = ((bf16[4,24,4608]{2,1,0:T(8,128)(2,1)}), bf16[4,24,4608]{2,1,0:T(8,128)(2,1)S(1)}, u32[]{:S(2)}, u32[]{:S(2)}) async-start(bf16[4,24,4608]{2,1,0:T(8,128)(2,1)} %broadcast_in_dim.8), calls=%async_computation.1 | async-start | bytes 1769472 | tf_op jit(solution)/shard_map/all_to_all | solution.py:35
  40.3 7.5 %collective-permute-start.2 = (bf16[96,192]{1,0:T(8,128)(2,1)S(1)}, bf16[96,192]{1,0:T(8,128)(2,1)S(1)}, u32[]{:S(2)}, u32[]{:S(2)}) collective-permute-start(bf16[96,192]{1,0:T(8,128)(2,1)S(1)} %pad_maximum_fusion), channel_id=1, source_target_pairs={{0,384},{96,480},{192,576},{288,672},{384,0},{480,96},{576,192},{6... | collective-permute-start | bytes 110600 | tf_op jit(solution)/shard_map/ppermute | solution.py:61
  48.0 4.7 %copy-start.5 = (bf16[192,192]{1,0:T(8,128)(2,1)}, bf16[192,192]{1,0:T(8,128)(2,1)S(1)}, u32[]{:S(2)}) copy-start(bf16[192,192]{1,0:T(8,128)(2,1)S(1)} %convolution_convert_fusion.2) | copy-start | bytes 221188
  48.4 4.3 %collective-permute-start.3 = (bf16[96,4608]{1,0:T(8,128)(2,1)S(1)}, bf16[96,4608]{1,0:T(8,128)(2,1)S(1)}, u32[]{:S(2)}, u32[]{:S(2)}) collective-permute-start(bf16[96,4608]{1,0:T(8,128)(2,1)S(1)} %convolution_convert_fusion.1), channel_id=1, source_target_pairs={{0,1},{1,0},{2,3},{3,2},{4,5},{5,4},{6,7},{7,6},{8,9},{9,8},{10,11... | collective-permute-start | bytes 2654216 | tf_op jit(solution)/shard_map/ppermute | solution.py:101
  54.4 21.0 %all-to-all-start.2 = ((bf16[4,24,4608]{2,1,0:T(8,128)(2,1)}), bf16[4,24,4608]{2,1,0:T(8,128)(2,1)S(1)}, u32[]{:S(2)}, u32[]{:S(2)}) async-start(bf16[4,24,4608]{2,1,0:T(8,128)(2,1)} %bitcast.1), calls=%async_computation.2 | async-start | bytes 1769472 | tf_op jit(solution)/shard_map/all_to_all | solution.py:35
  59.2 4.3 %collective-permute-start.4 = (bf16[96,4608]{1,0:T(8,128)(2,1)S(1)}, bf16[96,4608]{1,0:T(8,128)(2,1)S(1)}, u32[]{:S(2)}, u32[]{:S(2)}) collective-permute-start(bf16[96,4608]{1,0:T(8,128)(2,1)S(1)} %bitcast.14), channel_id=1, source_target_pairs={{0,1},{1,0},{2,3},{3,2},{4,5},{5,4},{6,7},{7,6},{8,9},{9,8},{10,11... | collective-permute-start | bytes 2654216 | tf_op jit(solution)/shard_map/ppermute | solution.py:108
  63.5 9.2 %copy-start.1 = (bf16[96,4608]{1,0:T(8,128)(2,1)}, bf16[96,4608]{1,0:T(8,128)(2,1)S(1)}, u32[]{:S(2)}) copy-start(bf16[96,4608]{1,0:T(8,128)(2,1)S(1)} %collective-permute-done.4) | copy-start | bytes 2654212
  64.5 7.5 %collective-permute-start.5 = (bf16[96,192]{1,0:T(8,128)(2,1)S(1)}, bf16[96,192]{1,0:T(8,128)(2,1)S(1)}, u32[]{:S(2)}, u32[]{:S(2)}) collective-permute-start(bf16[96,192]{1,0:T(8,128)(2,1)S(1)} %slice.153), channel_id=1, source_target_pairs={{0,384},{96,480},{192,576},{288,672},{384,0},{480,96},{576,192},{6... | collective-permute-start | bytes 110600 | tf_op jit(solution)/shard_map/ppermute | solution.py:68
  72.0 0.6 copy-start.3
  72.7 13.7 %collective-permute-start.6 = (bf16[48,192]{1,0:T(8,128)(2,1)}, bf16[48,192]{1,0:T(8,128)(2,1)}, u32[]{:S(2)}, u32[]{:S(2)}) collective-permute-start(bf16[48,192]{1,0:T(8,128)(2,1)} %slice.154), channel_id=1, source_target_pairs={{0,192},{96,288},{192,0},{288,96},{384,576},{480,672},{576,384},{6... | collective-permute-start | bytes 55304 | tf_op jit(solution)/shard_map/ppermute | solution.py:68
  78.1 21.6 %all-to-all-start.3 = ((bf16[12,2,4608]{2,1,0:T(2,128)(2,1)}), bf16[12,2,4608]{2,1,0:T(2,128)(2,1)S(1)}, u32[]{:S(2)}, u32[]{:S(2)}) async-start(bf16[12,2,4608]{2,1,0:T(2,128)(2,1)} %rev.3), calls=%async_computation.3 | async-start | bytes 442368 | tf_op jit(solution)/shard_map/all_to_all | solution.py:35
  87.2 12.5 %copy-start.2 = (f32[2,4608]{1,0:T(2,128)S(1)}, f32[2,4608]{1,0:T(2,128)}, u32[]{:S(2)}) copy-start(f32[2,4608]{1,0:T(2,128)} %get-tuple-element.11) | copy-start | bytes 110596
  87.2 12.5 %copy-start.4 = (bf16[2,4608]{1,0:T(2,128)(2,1)S(1)}, bf16[2,4608]{1,0:T(2,128)(2,1)}, u32[]{:S(2)}) copy-start(bf16[2,4608]{1,0:T(2,128)(2,1)} %param.6) | copy-start | bytes 55300
  87.2 13.2 %copy-start.6 = (bf16[2,4608]{1,0:T(2,128)(2,1)S(1)}, bf16[2,4608]{1,0:T(2,128)(2,1)}, u32[]{:S(2)}) copy-start(bf16[2,4608]{1,0:T(2,128)(2,1)} %param.7) | copy-start | bytes 55300
  87.3 9.7 %collective-permute-start.7 = (bf16[24,192]{1,0:T(8,128)(2,1)S(1)}, bf16[24,192]{1,0:T(8,128)(2,1)S(1)}, u32[]{:S(2)}, u32[]{:S(2)}) collective-permute-start(bf16[24,192]{1,0:T(8,128)(2,1)S(1)} %slice.155), channel_id=1, source_target_pairs={{0,96},{96,0},{192,288},{288,192},{384,480},{480,384},{576,672},{6... | collective-permute-start | bytes 27656 | tf_op jit(solution)/shard_map/ppermute | solution.py:68

commit v2 on v1

--- a/solution.py
+++ b/solution.py
@@ -17,18 +17,17 @@
 WIDE = [[dp_index(y, z, 0) for z in range(Z)] for y in range(YL)] + [
     [dp_index(y, n + NEAR * f, 1) for y in range(YL) for f in range(FAR)] for n in range(NEAR)
 ]
+BACK = [group[::-1] for group in WIDE]
 NARROW = [[dp_index(y, z, 0) for y in range(YL)] for z in range(Z)] + [
     [dp_index(y, n + NEAR * f, 1) for n in range(NEAR)] for y in range(YL) for f in range(FAR)
-]
-ORDER = [dp_index(y, z, 0) for y in range(YL) for z in range(Z)] + [
-    dp_index(y, n + NEAR * f, 1) for n in range(NEAR) for y in range(YL) for f in range(FAR)
 ]
 SWAP = [(i, i ^ 1) for i in range(YL * Z * C)]
 f32, bf16 = jnp.float32, jnp.bfloat16
 
 
-def row_order(each):
-    return np.array([[i * each + r for r in range(each)] for i in ORDER], np.int32).reshape(-1)
+def row_order(each, back):
+    order = [i for group in (BACK if back else WIDE) for i in group]
+    return np.array([[i * each + r for r in range(each)] for i in order], np.int32).reshape(-1)
 
 
 def exchange(blocks, groups):
@@ -49,8 +48,6 @@
 def tie(*arrays):
     return lax.optimization_barrier(arrays)
 
-BACK = [group[::-1] for group in WIDE]
-
 
 def partner(mask, members):
     return [(i, i ^ mask) for i in range(members)]
@@ -70,10 +67,10 @@
     return rows
 
 
-def placement(each, tokens):
+def placement(each, tokens, back):
     core = lax.axis_index("dp") % C
     mine = lax.axis_index("tensor")
-    rows = row_order(each)
+    rows = row_order(each, back)
     token_at = jnp.where(core == 0, rows, np.roll(rows, tokens // 2))
     column = jnp.arange(tokens, dtype=jnp.int32)
     own = tokens // 8
@@ -87,31 +84,36 @@
     tokens = own * 8
     half = tokens // 2
     few = half // 4
-    place = placement(each, tokens)
+    place = placement(each, tokens, False)
+    place_back = placement(each, tokens, True)
 
-    gate32 = gate.astype(f32)
-    up32 = up.astype(f32)
-    sigmoid = jax.nn.sigmoid(gate32)
-    silu = gate32 * sigmoid
-    hidden = (silu * up32).astype(bf16)
+    gate_in, up_in = (a.astype(f32) for a in tie(gate, up))
+    hidden = (gate_in * jax.nn.sigmoid(gate_in) * up_in).astype(bf16)
+    copies = jnp.broadcast_to(hidden[None], (12, each, units))
 
-    h1 = exchange(jnp.broadcast_to(hidden[None], (12, each, units)), WIDE).reshape(few, units)
+    h1 = exchange(copies, WIDE).reshape(few, units)
 
-    grads = dot(place, gather_tokens(out_grad), 1, 0).astype(bf16)
+    rows = gather_tokens(out_grad)
+    grads = dot(place_back, rows, 1, 0).astype(bf16)
     received = lax.ppermute(dot(grads[half:], down_weight, 1, 1).astype(bf16), "dp", SWAP)
     r1 = (dot(grads[:half], down_weight, 1, 1) + received.astype(f32)).astype(bf16)
 
     h2 = exchange(jnp.broadcast_to(h1[None], (4, few, units)), NARROW).reshape(half, units)
     h2, r1 = tie(h2, r1)
     r2 = total(exchange(r1.reshape(4, few, units), NARROW)).astype(bf16).reshape(12, each, units)
-    r3 = exchange(r2[::-1], BACK)
+    r3 = exchange(r2, BACK)
     other = lax.ppermute(h2, "dp", SWAP)
     partial_out = jnp.concatenate(
         [dot(h2, down_weight, 1, 0).astype(bf16), dot(other, down_weight, 1, 0).astype(bf16)], axis=0
     )
     output = scatter_tokens(dot(place, partial_out, 0, 0)).astype(bf16)
 
+    gate32 = gate.astype(f32)
+    up32 = up.astype(f32)
+    sigmoid = jax.nn.sigmoid(gate32)
+    silu = gate32 * sigmoid
     hidden_grad = total(r3)
+    grads = dot(place, rows, 1, 0).astype(bf16)
     grad_down = dot(jnp.concatenate([h2, other], axis=0), grads, 0, 0).astype(bf16)
     grad_gate = (hidden_grad * up32 * sigmoid * (1.0 + gate32 * (1.0 - sigmoid))).astype(bf16)
     grad_up = (hidden_grad * silu).astype(bf16)

time: 102 us -> 101 us (level)
  waiting for transfers between devices: 19.5 us -> 18.1 us
    ppermute x3, waiting for transfers between devices: 6.1 us -> 4.68 us  [gather_tokens(): lax.ppermute(rows, 'tensor', partner(mask, 8))]
  transfers between devices with their start and end apart: 12 -> 12, of which waited for: 8 -> 8; matrix products, arithmetic and copies ran while one was open for 13% -> 15% of each run, Pallas kernels for 0% -> 0%
where the time goes in v2:
time: 101 us
  starting transfers between devices  63.5 us (63%)
  waiting for transfers between devices  18.1 us (18%)
  matrix products  6.92 us (7%)
  other arithmetic  6.03 us (6%)
  local copies, waits for them, and re-layouts  5 us (5%)
    all_to_all x4, starting transfers between devices, exchange(): return lax.all_to_all(blocks, 'dp', 0, 0, axis_index_groups=groups)  33.4 us
    ppermute x3, starting transfers between devices, gather_tokens(): lax.ppermute(rows, 'tensor', partner(mask, 8))  13.8 us
    ppermute x3, starting transfers between devices, scatter_tokens(): theirs = lax.ppermute(rows[half:].astype(bf16), 'tensor', partner(mask, 8))  12.6 us
    dot_general x7, matrix products, dot(): lax.dot_general(a, b, (((ca,), (cb,)), ((), ())), preferred_element_type=...  6.92 us
    all_to_all x4, waiting for transfers between devices, exchange(): return lax.all_to_all(blocks, 'dp', 0, 0, axis_index_groups=groups)  5.23 us
    ppermute x3, waiting for transfers between devices, gather_tokens(): lax.ppermute(rows, 'tensor', partner(mask, 8))  4.68 us
    ppermute x3, waiting for transfers between devices, scatter_tokens(): theirs = lax.ppermute(rows[half:].astype(bf16), 'tensor', partner(mask, 8))  4.17 us
    ppermute x1, waiting for transfers between devices, local(): lax.ppermute(dot(grads[half:], down_weight, 1, 1).astype(bf16), 'dp', SWAP)  2.39 us
  transfers between devices with their start and end apart: 12, of which 8 were waited for; matrix products, arithmetic and copies ran while one was open for 15% of the time, Pallas kernels for 0%

profile of v2, /device:TPU:6, one launch (start us, length us, event | category | flops | bytes accessed | tf_op | source)
XLA Modules:
  0.0 100.5 jit_solution(5268983929749458092)
XLA Ops:
  0.6 0.0 copy-start
  0.6 0.9 fusion.36
  1.6 0.8 broadcast_in_dim.6
  2.4 15.2 %all-to-all-start = ((bf16[12,2,4608]{2,1,0:T(2,128)(2,1)}), bf16[12,2,4608]{2,1,0:T(2,128)(2,1)S(1)}, u32[]{:S(2)}, u32[]{:S(2)}) async-start(bf16[12,2,4608]{2,1,0:T(2,128)(2,1)} %broadcast_in_dim.6), calls=%async_computation | async-start | bytes 442368 | tf_op jit(solution)/shard_map/all_to_all | solution.py:34
  17.5 0.0 copy-start.5
  17.6 7.7 %collective-permute-start = (bf16[24,192]{1,0:T(8,128)(2,1)}, bf16[24,192]{1,0:T(8,128)(2,1)S(1)}, u32[]{:S(2)}, u32[]{:S(2)}) collective-permute-start(bf16[24,192]{1,0:T(8,128)(2,1)} %param.11), channel_id=1, source_target_pairs={{0,96},{96,0},{192,288},{288,192},{384,480},{480,384},{576,672},{6... | collective-permute-start | bytes 27656 | tf_op jit(solution)/shard_map/ppermute | solution.py:58
  25.3 0.7 fusion.40
  26.0 0.7 constant_dynamic-update-slice_fusion.3
  26.7 0.5 collective-permute-done
  27.3 0.7 pad_maximum_fusion.1
  28.0 2.7 %collective-permute-start.1 = (bf16[48,192]{1,0:T(8,128)(2,1)S(1)}, bf16[48,192]{1,0:T(8,128)(2,1)S(1)}, u32[]{:S(2)}, u32[]{:S(2)}) collective-permute-start(bf16[48,192]{1,0:T(8,128)(2,1)S(1)} %pad_maximum_fusion.1), channel_id=1, source_target_pairs={{0,192},{96,288},{192,0},{288,96},{384,576},{480,672},{576,384},{6... | collective-permute-start | bytes 55304 | tf_op jit(solution)/shard_map/ppermute | solution.py:58
  30.7 2.9 %all-to-all-done = bf16[12,2,4608]{2,1,0:T(2,128)(2,1)S(1)} async-done(((bf16[12,2,4608]{2,1,0:T(2,128)(2,1)}), bf16[12,2,4608]{2,1,0:T(2,128)(2,1)S(1)}, u32[]{:S(2)}, u32[]{:S(2)}) %all-to-all-start) | async-done | bytes 221216 | tf_op jit(solution)/shard_map/all_to_all | solution.py:34
  33.6 0.1 broadcast_in_dim.7
  33.7 1.0 broadcast_in_dim.8
  34.6 5.0 %all-to-all-start.1 = ((bf16[4,24,4608]{2,1,0:T(8,128)(2,1)}), bf16[4,24,4608]{2,1,0:T(8,128)(2,1)S(1)}, u32[]{:S(2)}, u32[]{:S(2)}) async-start(bf16[4,24,4608]{2,1,0:T(8,128)(2,1)} %broadcast_in_dim.8), calls=%async_computation.1 | async-start | bytes 1769472 | tf_op jit(solution)/shard_map/all_to_all | solution.py:34
  39.6 0.0 collective-permute-done.1
  39.6 0.0 copy-done.5
  39.7 3.3 %collective-permute-start.2 = (bf16[96,192]{1,0:T(8,128)(2,1)S(1)}, bf16[96,192]{1,0:T(8,128)(2,1)S(1)}, u32[]{:S(2)}, u32[]{:S(2)}) collective-permute-start(bf16[96,192]{1,0:T(8,128)(2,1)S(1)} %pad_maximum_fusion), channel_id=1, source_target_pairs={{0,384},{96,480},{192,576},{288,672},{384,0},{480,96},{576,192},{6... | collective-permute-start | bytes 110600 | tf_op jit(solution)/shard_map/ppermute | solution.py:58
  43.0 4.2 %collective-permute-done.2 = bf16[96,192]{1,0:T(8,128)(2,1)S(1)} collective-permute-done((bf16[96,192]{1,0:T(8,128)(2,1)S(1)}, bf16[96,192]{1,0:T(8,128)(2,1)S(1)}, u32[]{:S(2)}, u32[]{:S(2)}) %collective-permute-start.2) | collective-permute-done | bytes 36896 | tf_op jit(solution)/shard_map/ppermute | solution.py:58
  47.2 0.0 copy-start.4
  47.2 0.2 convolution_convert_fusion.3
  47.4 0.0 copy-done
  47.4 0.4 convolution_convert_fusion.1
  47.8 1.9 %collective-permute-start.3 = (bf16[96,4608]{1,0:T(8,128)(2,1)S(1)}, bf16[96,4608]{1,0:T(8,128)(2,1)S(1)}, u32[]{:S(2)}, u32[]{:S(2)}) collective-permute-start(bf16[96,4608]{1,0:T(8,128)(2,1)S(1)} %convolution_convert_fusion.1), channel_id=1, source_target_pairs={{0,1},{1,0},{2,3},{3,2},{4,5},{5,4},{6,7},{7,6},{8,9},{9,8},{10,11... | collective-permute-start | bytes 2654216 | tf_op jit(solution)/shard_map/ppermute | solution.py:98
  49.7 2.4 %collective-permute-done.3 = bf16[96,4608]{1,0:T(8,128)(2,1)S(1)} collective-permute-done((bf16[96,4608]{1,0:T(8,128)(2,1)S(1)}, bf16[96,4608]{1,0:T(8,128)(2,1)S(1)}, u32[]{:S(2)}, u32[]{:S(2)}) %collective-permute-start.3) | collective-permute-done | bytes 884768 | tf_op jit(solution)/shard_map/ppermute | solution.py:98
  52.1 1.4 %add_convert_fusion = bf16[96,4608]{1,0:T(8,128)(2,1)} fusion(bf16[96,4608]{1,0:T(8,128)(2,1)S(1)} %collective-permute-done.3, bf16[4608,192]{0,1:T(8,128)(2,1)S(1)} %copy-done, bf16[192,192]{1,0:T(8,128)(2,1)S(1)} %convolution_convert_fusion.3), kind=kOutput, calls=%fused_computation.5 | convolution fusion | flops 171196416 | bytes 3588096 | tf_op jit(solution)/shard_map/dot_general | solution.py:45
  53.5 0.0 copy-done.4
  53.5 0.0 copy-start.7
  53.5 0.0 copy-start.8
  53.5 0.3 all-to-all-done.1
  53.8 4.9 %all-to-all-start.2 = ((bf16[4,24,4608]{2,1,0:T(8,128)(2,1)}), bf16[4,24,4608]{2,1,0:T(8,128)(2,1)S(1)}, u32[]{:S(2)}, u32[]{:S(2)}) async-start(bf16[4,24,4608]{2,1,0:T(8,128)(2,1)} %bitcast.1), calls=%async_computation.2 | async-start | bytes 1769472 | tf_op jit(solution)/shard_map/all_to_all | solution.py:34
  58.7 1.9 %collective-permute-start.4 = (bf16[96,4608]{1,0:T(8,128)(2,1)S(1)}, bf16[96,4608]{1,0:T(8,128)(2,1)S(1)}, u32[]{:S(2)}, u32[]{:S(2)}) collective-permute-start(bf16[96,4608]{1,0:T(8,128)(2,1)S(1)} %bitcast.17), channel_id=1, source_target_pairs={{0,1},{1,0},{2,3},{3,2},{4,5},{5,4},{6,7},{7,6},{8,9},{9,8},{10,11... | collective-permute-start | bytes 2654216 | tf_op jit(solution)/shard_map/ppermute | solution.py:105
  60.6 0.0 copy-done.7
  60.7 0.0 copy-done.8
  60.7 0.7 convolution_convert_fusion.5
  61.4 1.7 %collective-permute-done.4 = bf16[96,4608]{1,0:T(8,128)(2,1)S(1)} collective-permute-done((bf16[96,4608]{1,0:T(8,128)(2,1)S(1)}, bf16[96,4608]{1,0:T(8,128)(2,1)S(1)}, u32[]{:S(2)}, u32[]{:S(2)}) %collective-permute-start.4) | collective-permute-done | bytes 884768 | tf_op jit(solution)/shard_map/ppermute | solution.py:105
  63.0 0.0 copy-start.1
  63.0 0.7 convolution_convert_fusion.4
  63.7 0.3 fusion.5
  64.1 3.3 %collective-permute-start.5 = (bf16[96,192]{1,0:T(8,128)(2,1)S(1)}, bf16[96,192]{1,0:T(8,128)(2,1)S(1)}, u32[]{:S(2)}, u32[]{:S(2)}) collective-permute-start(bf16[96,192]{1,0:T(8,128)(2,1)S(1)} %slice.153), channel_id=1, source_target_pairs={{0,384},{96,480},{192,576},{288,672},{384,0},{480,96},{576,192},{6... | collective-permute-start | bytes 110600 | tf_op jit(solution)/shard_map/ppermute | solution.py:65
  67.4 4.2 %collective-permute-done.5 = bf16[96,192]{1,0:T(8,128)(2,1)S(1)} collective-permute-done((bf16[96,192]{1,0:T(8,128)(2,1)S(1)}, bf16[96,192]{1,0:T(8,128)(2,1)S(1)}, u32[]{:S(2)}, u32[]{:S(2)}) %collective-permute-start.5) | collective-permute-done | bytes 36896 | tf_op jit(solution)/shard_map/ppermute | solution.py:65
  71.6 0.0 copy-start.2
  71.6 0.7 slice.154
  72.2 0.0 copy-done.1
  72.2 0.0 copy-done.2
  72.2 2.7 %collective-permute-start.6 = (bf16[48,192]{1,0:T(8,128)(2,1)}, bf16[48,192]{1,0:T(8,128)(2,1)}, u32[]{:S(2)}, u32[]{:S(2)}) collective-permute-start(bf16[48,192]{1,0:T(8,128)(2,1)} %slice.154), channel_id=1, source_target_pairs={{0,192},{96,288},{192,0},{288,96},{384,576},{480,672},{576,384},{6... | collective-permute-start | bytes 55304 | tf_op jit(solution)/shard_map/ppermute | solution.py:65
  75.0 0.0 all-to-all-done.2
  75.0 0.8 add_convert_fusion.1
  75.8 1.7 %convert_element_type.157 = bf16[12,2,4608]{2,1,0:T(2,128)(2,1)} reshape(bf16[1,24,4608]{2,1,0:T(8,128)(2,1)} %add_convert_fusion.1) | data formatting | bytes 442368 | tf_op jit(solution)/shard_map/convert_element_type | solution.py:103
  77.5 8.3 %all-to-all-start.3 = ((bf16[12,2,4608]{2,1,0:T(2,128)(2,1)}), bf16[12,2,4608]{2,1,0:T(2,128)(2,1)S(1)}, u32[]{:S(2)}, u32[]{:S(2)}) async-start(bf16[12,2,4608]{2,1,0:T(2,128)(2,1)} %convert_element_type.157), calls=%async_computation.3 | async-start | bytes 442368 | tf_op jit(solution)/shard_map/all_to_all | solution.py:34
  85.8 0.0 collective-permute-done.6
  85.8 0.8 slice_add_fusion.1
  86.6 0.0 copy-start.3
  86.6 0.0 copy-start.6
  86.6 6.5 %collective-permute-start.7 = (bf16[24,192]{1,0:T(8,128)(2,1)S(1)}, bf16[24,192]{1,0:T(8,128)(2,1)S(1)}, u32[]{:S(2)}, u32[]{:S(2)}) collective-permute-start(bf16[24,192]{1,0:T(8,128)(2,1)S(1)} %slice.155), channel_id=1, source_target_pairs={{0,96},{96,0},{192,288},{288,192},{384,480},{480,384},{576,672},{6... | collective-permute-start | bytes 27656 | tf_op jit(solution)/shard_map/ppermute | solution.py:65
  93.1 3.3 %convolution_convert_fusion = bf16[4608,192]{0,1:T(8,128)(2,1)} fusion(bf16[96,4608]{1,0:T(8,128)(2,1)} %copy-done.1, bf16[96,4608]{1,0:T(8,128)(2,1)S(1)} %bitcast.19, bf16[192,192]{1,0:T(8,128)(2,1)} %copy-done.4, s32[192]{0:T(256)S(1)} %get-tuple-element.14, s32[192]{0:T(256)S(1)} %broadcast_select_fusion.1), kind=kOutput, calls=%fused_computation | convolution fusion | flops 358391808 | bytes 3614208 | tf_op jit(solution)/shard_map/dot_general | solution.py:45
  96.4 0.0 collective-permute-done.7
  96.4 0.6 fusion.37
  97.0 2.1 %all-to-all-done.3 = bf16[12,2,4608]{2,1,0:T(2,128)(2,1)S(1)} async-done(((bf16[12,2,4608]{2,1,0:T(2,128)(2,1)}), bf16[12,2,4608]{2,1,0:T(2,128)(2,1)S(1)}, u32[]{:S(2)}, u32[]{:S(2)}) %all-to-all-start.3) | async-done | bytes 221216 | tf_op jit(solution)/shard_map/all_to_all | solution.py:34
  99.1 0.0 copy-done.3
  99.1 0.8 fusion.34
  99.8 0.0 copy-done.6
  99.8 0.7 fusion.32
  (8 shorter events, 0.1 us)
Async XLA Ops:
  0.6 46.8 %copy-start = (bf16[4608,192]{0,1:T(8,128)(2,1)S(1)}, bf16[4608,192]{0,1:T(8,128)(2,1)}, u32[]{:S(2)}) copy-start(bf16[4608,192]{0,1:T(8,128)(2,1)} %param.10) | copy-start | bytes 5308420
  2.4 31.2 %all-to-all-start = ((bf16[12,2,4608]{2,1,0:T(2,128)(2,1)}), bf16[12,2,4608]{2,1,0:T(2,128)(2,1)S(1)}, u32[]{:S(2)}, u32[]{:S(2)}) async-start(bf16[12,2,4608]{2,1,0:T(2,128)(2,1)} %broadcast_in_dim.6), calls=%async_computation | async-start | bytes 442368 | tf_op jit(solution)/shard_map/all_to_all | solution.py:34
  17.5 22.1 %copy-start.5 = (bf16[24,192]{1,0:T(8,128)(2,1)S(1)}, bf16[24,192]{1,0:T(8,128)(2,1)}, u32[]{:S(2)}) copy-start(bf16[24,192]{1,0:T(8,128)(2,1)} %param.11) | copy-start | bytes 27652
  17.6 9.7 %collective-permute-start = (bf16[24,192]{1,0:T(8,128)(2,1)}, bf16[24,192]{1,0:T(8,128)(2,1)S(1)}, u32[]{:S(2)}, u32[]{:S(2)}) collective-permute-start(bf16[24,192]{1,0:T(8,128)(2,1)} %param.11), channel_id=1, source_target_pairs={{0,96},{96,0},{192,288},{288,192},{384,480},{480,384},{576,672},{6... | collective-permute-start | bytes 27656 | tf_op jit(solution)/shard_map/ppermute | solution.py:58
  28.0 11.7 %collective-permute-start.1 = (bf16[48,192]{1,0:T(8,128)(2,1)S(1)}, bf16[48,192]{1,0:T(8,128)(2,1)S(1)}, u32[]{:S(2)}, u32[]{:S(2)}) collective-permute-start(bf16[48,192]{1,0:T(8,128)(2,1)S(1)} %pad_maximum_fusion.1), channel_id=1, source_target_pairs={{0,192},{96,288},{192,0},{288,96},{384,576},{480,672},{576,384},{6... | collective-permute-start | bytes 55304 | tf_op jit(solution)/shard_map/ppermute | solution.py:58
  34.6 19.2 %all-to-all-start.1 = ((bf16[4,24,4608]{2,1,0:T(8,128)(2,1)}), bf16[4,24,4608]{2,1,0:T(8,128)(2,1)S(1)}, u32[]{:S(2)}, u32[]{:S(2)}) async-start(bf16[4,24,4608]{2,1,0:T(8,128)(2,1)} %broadcast_in_dim.8), calls=%async_computation.1 | async-start | bytes 1769472 | tf_op jit(solution)/shard_map/all_to_all | solution.py:34
  39.7 7.5 %collective-permute-start.2 = (bf16[96,192]{1,0:T(8,128)(2,1)S(1)}, bf16[96,192]{1,0:T(8,128)(2,1)S(1)}, u32[]{:S(2)}, u32[]{:S(2)}) collective-permute-start(bf16[96,192]{1,0:T(8,128)(2,1)S(1)} %pad_maximum_fusion), channel_id=1, source_target_pairs={{0,384},{96,480},{192,576},{288,672},{384,0},{480,96},{576,192},{6... | collective-permute-start | bytes 110600 | tf_op jit(solution)/shard_map/ppermute | solution.py:58
  47.2 6.3 %copy-start.4 = (bf16[192,192]{1,0:T(8,128)(2,1)}, bf16[192,192]{1,0:T(8,128)(2,1)S(1)}, u32[]{:S(2)}) copy-start(bf16[192,192]{1,0:T(8,128)(2,1)S(1)} %constant_dynamic-update-slice_fusion) | copy-start | bytes 221188
  47.8 4.3 %collective-permute-start.3 = (bf16[96,4608]{1,0:T(8,128)(2,1)S(1)}, bf16[96,4608]{1,0:T(8,128)(2,1)S(1)}, u32[]{:S(2)}, u32[]{:S(2)}) collective-permute-start(bf16[96,4608]{1,0:T(8,128)(2,1)S(1)} %convolution_convert_fusion.1), channel_id=1, source_target_pairs={{0,1},{1,0},{2,3},{3,2},{4,5},{5,4},{6,7},{7,6},{8,9},{9,8},{10,11... | collective-permute-start | bytes 2654216 | tf_op jit(solution)/shard_map/ppermute | solution.py:98
  53.5 7.2 %copy-start.7 = (s32[192]{0:T(256)S(1)}, s32[192]{0:T(256)}, u32[]{:S(2)}) copy-start(s32[192]{0:T(256)} %constant.57.clone) | copy-start | bytes 2308
  53.5 7.2 %copy-start.8 = (s32[192]{0:T(256)S(1)}, s32[192]{0:T(256)}, u32[]{:S(2)}) copy-start(s32[192]{0:T(256)} %constant.56.clone) | copy-start | bytes 2308
  53.8 21.2 %all-to-all-start.2 = ((bf16[4,24,4608]{2,1,0:T(8,128)(2,1)}), bf16[4,24,4608]{2,1,0:T(8,128)(2,1)S(1)}, u32[]{:S(2)}, u32[]{:S(2)}) async-start(bf16[4,24,4608]{2,1,0:T(8,128)(2,1)} %bitcast.1), calls=%async_computation.2 | async-start | bytes 1769472 | tf_op jit(solution)/shard_map/all_to_all | solution.py:34
  58.7 4.3 %collective-permute-start.4 = (bf16[96,4608]{1,0:T(8,128)(2,1)S(1)}, bf16[96,4608]{1,0:T(8,128)(2,1)S(1)}, u32[]{:S(2)}, u32[]{:S(2)}) collective-permute-start(bf16[96,4608]{1,0:T(8,128)(2,1)S(1)} %bitcast.17), channel_id=1, source_target_pairs={{0,1},{1,0},{2,3},{3,2},{4,5},{5,4},{6,7},{7,6},{8,9},{9,8},{10,11... | collective-permute-start | bytes 2654216 | tf_op jit(solution)/shard_map/ppermute | solution.py:105
  63.0 9.2 %copy-start.1 = (bf16[96,4608]{1,0:T(8,128)(2,1)}, bf16[96,4608]{1,0:T(8,128)(2,1)S(1)}, u32[]{:S(2)}) copy-start(bf16[96,4608]{1,0:T(8,128)(2,1)S(1)} %collective-permute-done.4) | copy-start | bytes 2654212
  64.1 7.5 %collective-permute-start.5 = (bf16[96,192]{1,0:T(8,128)(2,1)S(1)}, bf16[96,192]{1,0:T(8,128)(2,1)S(1)}, u32[]{:S(2)}, u32[]{:S(2)}) collective-permute-start(bf16[96,192]{1,0:T(8,128)(2,1)S(1)} %slice.153), channel_id=1, source_target_pairs={{0,384},{96,480},{192,576},{288,672},{384,0},{480,96},{576,192},{6... | collective-permute-start | bytes 110600 | tf_op jit(solution)/shard_map/ppermute | solution.py:65
  71.6 0.7 copy-start.2
  72.2 13.5 %collective-permute-start.6 = (bf16[48,192]{1,0:T(8,128)(2,1)}, bf16[48,192]{1,0:T(8,128)(2,1)}, u32[]{:S(2)}, u32[]{:S(2)}) collective-permute-start(bf16[48,192]{1,0:T(8,128)(2,1)} %slice.154), channel_id=1, source_target_pairs={{0,192},{96,288},{192,0},{288,96},{384,576},{480,672},{576,384},{6... | collective-permute-start | bytes 55304 | tf_op jit(solution)/shard_map/ppermute | solution.py:65
  77.5 21.6 %all-to-all-start.3 = ((bf16[12,2,4608]{2,1,0:T(2,128)(2,1)}), bf16[12,2,4608]{2,1,0:T(2,128)(2,1)S(1)}, u32[]{:S(2)}, u32[]{:S(2)}) async-start(bf16[12,2,4608]{2,1,0:T(2,128)(2,1)} %convert_element_type.157), calls=%async_computation.3 | async-start | bytes 442368 | tf_op jit(solution)/shard_map/all_to_all | solution.py:34
  86.6 12.5 %copy-start.3 = (bf16[2,4608]{1,0:T(2,128)(2,1)S(1)}, bf16[2,4608]{1,0:T(2,128)(2,1)}, u32[]{:S(2)}) copy-start(bf16[2,4608]{1,0:T(2,128)(2,1)} %param.8) | copy-start | bytes 55300
  86.6 13.3 %copy-start.6 = (bf16[2,4608]{1,0:T(2,128)(2,1)S(1)}, bf16[2,4608]{1,0:T(2,128)(2,1)}, u32[]{:S(2)}) copy-start(bf16[2,4608]{1,0:T(2,128)(2,1)} %param.9) | copy-start | bytes 55300
  86.6 9.8 %collective-permute-start.7 = (bf16[24,192]{1,0:T(8,128)(2,1)S(1)}, bf16[24,192]{1,0:T(8,128)(2,1)S(1)}, u32[]{:S(2)}, u32[]{:S(2)}) collective-permute-start(bf16[24,192]{1,0:T(8,128)(2,1)S(1)} %slice.155), channel_id=1, source_target_pairs={{0,96},{96,0},{192,288},{288,192},{384,480},{480,384},{576,672},{6... | collective-permute-start | bytes 27656 | tf_op jit(solution)/shard_map/ppermute | solution.py:65

commit v3 on v2

--- a/solution.py
+++ b/solution.py
@@ -3,6 +3,8 @@
 import jax
 import jax.numpy as jnp
 from jax import lax
+from jax.experimental import pallas as pl
+from jax.experimental.pallas import tpu as pltpu
 from jax.sharding import PartitionSpec as P
 
 YL, Z, C = 4, 12, 2
@@ -43,6 +45,27 @@
 
 def dot(a, b, ca, cb):
     return lax.dot_general(a, b, (((ca,), (cb,)), ((), ())), preferred_element_type=f32)
+
+
+def fold_kernel(blocks_ref, out_ref):
+    sums = total(blocks_ref)
+    each = out_ref.shape[1]
+    for j in range(out_ref.shape[0]):
+        out_ref[j] = sums[j * each : (j + 1) * each].astype(bf16)
+
+
+def fold(blocks, each):
+    count, few, units = blocks.shape
+    return pl.pallas_call(
+        fold_kernel,
+        in_specs=[pl.BlockSpec(memory_space=pltpu.VMEM)],
+        out_specs=pl.BlockSpec(memory_space=pltpu.VMEM),
+        out_shape=jax.ShapeDtypeStruct((few // each, each, units), bf16),
+        compiler_params=pltpu.CompilerParams(vmem_limit_bytes=8 * 2**20),
+        cost_estimate=pl.CostEstimate(
+            flops=blocks.size, bytes_accessed=2 * blocks.size + 2 * few * units, transcendentals=0
+        ),
+    )(blocks)
 
 
 def tie(*arrays):
@@ -100,7 +123,7 @@
 
     h2 = exchange(jnp.broadcast_to(h1[None], (4, few, units)), NARROW).reshape(half, units)
     h2, r1 = tie(h2, r1)
-    r2 = total(exchange(r1.reshape(4, few, units), NARROW)).astype(bf16).reshape(12, each, units)
+    r2 = fold(exchange(r1.reshape(4, few, units), NARROW), each)
     r3 = exchange(r2, BACK)
     other = lax.ppermute(h2, "dp", SWAP)
     partial_out = jnp.concatenate(

time: 101 us -> 99.8 us (0.988)
  local copies, waits for them, and re-layouts: 5 us -> 3.27 us
    convert_element_type x1 -> x0, local copies, waits for them, and re-layouts: 1.72 us -> none  [local(): total(exchange(r1.reshape(4, few, units), NARROW)).astype(bf16)]
  transfers between devices with their start and end apart: 12 -> 12, of which waited for: 8 -> 8; matrix products, arithmetic and copies ran while one was open for 15% -> 12% of each run, Pallas kernels for 0% -> 1%
where the time goes in v3:
time: 99.8 us; the launch traced here: 98.8 us
  starting transfers between devices  63.5 us (64%)
  waiting for transfers between devices  18.1 us (18%)
  matrix products  6.92 us (7%)
  other arithmetic  5.23 us (5%)
  local copies, waits for them, and re-layouts  3.27 us (3%)
    all_to_all x4, starting transfers between devices, exchange(): return lax.all_to_all(blocks, 'dp', 0, 0, axis_index_groups=groups)  33.4 us
    ppermute x3, starting transfers between devices, gather_tokens(): lax.ppermute(rows, 'tensor', partner(mask, 8))  13.8 us
    ppermute x3, starting transfers between devices, scatter_tokens(): theirs = lax.ppermute(rows[half:].astype(bf16), 'tensor', partner(mask, 8))  12.6 us
    dot_general x7, matrix products, dot(): lax.dot_general(a, b, (((ca,), (cb,)), ((), ())), preferred_element_type=...  6.92 us
    all_to_all x4, waiting for transfers between devices, exchange(): return lax.all_to_all(blocks, 'dp', 0, 0, axis_index_groups=groups)  5.23 us
    ppermute x3, waiting for transfers between devices, gather_tokens(): lax.ppermute(rows, 'tensor', partner(mask, 8))  4.68 us
    ppermute x3, waiting for transfers between devices, scatter_tokens(): theirs = lax.ppermute(rows[half:].astype(bf16), 'tensor', partner(mask, 8))  4.17 us
    ppermute x1, waiting for transfers between devices, local(): lax.ppermute(dot(grads[half:], down_weight, 1, 1).astype(bf16), 'dp', SWAP)  2.39 us
  transfers between devices with their start and end apart: 12, of which 8 were waited for; matrix products, arithmetic and copies ran while one was open for 12% of the time, Pallas kernels for 1%

profile of v3, /device:TPU:6, one launch (start us, length us, event | category | flops | bytes accessed | tf_op | source)
XLA Modules:
  0.0 98.8 jit_solution(12106848510350738976)
XLA Ops:
  0.6 0.0 copy-start
  0.6 0.9 fusion.36
  1.6 0.8 broadcast_in_dim.6
  2.4 15.2 %all-to-all-start = ((bf16[12,2,4608]{2,1,0:T(2,128)(2,1)}), bf16[12,2,4608]{2,1,0:T(2,128)(2,1)S(1)}, u32[]{:S(2)}, u32[]{:S(2)}) async-start(bf16[12,2,4608]{2,1,0:T(2,128)(2,1)} %broadcast_in_dim.6), calls=%async_computation | async-start | bytes 442368 | tf_op jit(solution)/shard_map/all_to_all | solution.py:36
  17.5 0.0 copy-start.5
  17.6 7.7 %collective-permute-start = (bf16[24,192]{1,0:T(8,128)(2,1)}, bf16[24,192]{1,0:T(8,128)(2,1)S(1)}, u32[]{:S(2)}, u32[]{:S(2)}) collective-permute-start(bf16[24,192]{1,0:T(8,128)(2,1)} %param.11), channel_id=1, source_target_pairs={{0,96},{96,0},{192,288},{288,192},{384,480},{480,384},{576,672},{6... | collective-permute-start | bytes 27656 | tf_op jit(solution)/shard_map/ppermute | solution.py:81
  25.3 0.7 fusion.40
  26.0 0.7 constant_dynamic-update-slice_fusion.3
  26.7 0.5 collective-permute-done
  27.3 0.7 pad_maximum_fusion.1
  28.0 2.7 %collective-permute-start.1 = (bf16[48,192]{1,0:T(8,128)(2,1)S(1)}, bf16[48,192]{1,0:T(8,128)(2,1)S(1)}, u32[]{:S(2)}, u32[]{:S(2)}) collective-permute-start(bf16[48,192]{1,0:T(8,128)(2,1)S(1)} %pad_maximum_fusion.1), channel_id=1, source_target_pairs={{0,192},{96,288},{192,0},{288,96},{384,576},{480,672},{576,384},{6... | collective-permute-start | bytes 55304 | tf_op jit(solution)/shard_map/ppermute | solution.py:81
  30.7 2.9 %all-to-all-done = bf16[12,2,4608]{2,1,0:T(2,128)(2,1)S(1)} async-done(((bf16[12,2,4608]{2,1,0:T(2,128)(2,1)}), bf16[12,2,4608]{2,1,0:T(2,128)(2,1)S(1)}, u32[]{:S(2)}, u32[]{:S(2)}) %all-to-all-start) | async-done | bytes 221216 | tf_op jit(solution)/shard_map/all_to_all | solution.py:36
  33.6 0.1 broadcast_in_dim.7
  33.7 1.0 broadcast_in_dim.8
  34.6 5.0 %all-to-all-start.1 = ((bf16[4,24,4608]{2,1,0:T(8,128)(2,1)}), bf16[4,24,4608]{2,1,0:T(8,128)(2,1)S(1)}, u32[]{:S(2)}, u32[]{:S(2)}) async-start(bf16[4,24,4608]{2,1,0:T(8,128)(2,1)} %broadcast_in_dim.8), calls=%async_computation.1 | async-start | bytes 1769472 | tf_op jit(solution)/shard_map/all_to_all | solution.py:36
  39.6 0.0 collective-permute-done.1
  39.6 0.0 copy-done.5
  39.7 3.3 %collective-permute-start.2 = (bf16[96,192]{1,0:T(8,128)(2,1)S(1)}, bf16[96,192]{1,0:T(8,128)(2,1)S(1)}, u32[]{:S(2)}, u32[]{:S(2)}) collective-permute-start(bf16[96,192]{1,0:T(8,128)(2,1)S(1)} %pad_maximum_fusion), channel_id=1, source_target_pairs={{0,384},{96,480},{192,576},{288,672},{384,0},{480,96},{576,192},{6... | collective-permute-start | bytes 110600 | tf_op jit(solution)/shard_map/ppermute | solution.py:81
  43.0 4.2 %collective-permute-done.2 = bf16[96,192]{1,0:T(8,128)(2,1)S(1)} collective-permute-done((bf16[96,192]{1,0:T(8,128)(2,1)S(1)}, bf16[96,192]{1,0:T(8,128)(2,1)S(1)}, u32[]{:S(2)}, u32[]{:S(2)}) %collective-permute-start.2) | collective-permute-done | bytes 36896 | tf_op jit(solution)/shard_map/ppermute | solution.py:81
  47.2 0.0 copy-start.4
  47.2 0.2 convolution_convert_fusion.3
  47.4 0.0 copy-done
  47.4 0.4 convolution_convert_fusion.1
  47.8 1.9 %collective-permute-start.3 = (bf16[96,4608]{1,0:T(8,128)(2,1)S(1)}, bf16[96,4608]{1,0:T(8,128)(2,1)S(1)}, u32[]{:S(2)}, u32[]{:S(2)}) collective-permute-start(bf16[96,4608]{1,0:T(8,128)(2,1)S(1)} %convolution_convert_fusion.1), channel_id=1, source_target_pairs={{0,1},{1,0},{2,3},{3,2},{4,5},{5,4},{6,7},{7,6},{8,9},{9,8},{10,11... | collective-permute-start | bytes 2654216 | tf_op jit(solution)/shard_map/ppermute | solution.py:121
  49.7 2.4 %collective-permute-done.3 = bf16[96,4608]{1,0:T(8,128)(2,1)S(1)} collective-permute-done((bf16[96,4608]{1,0:T(8,128)(2,1)S(1)}, bf16[96,4608]{1,0:T(8,128)(2,1)S(1)}, u32[]{:S(2)}, u32[]{:S(2)}) %collective-permute-start.3) | collective-permute-done | bytes 884768 | tf_op jit(solution)/shard_map/ppermute | solution.py:121
  52.1 1.4 %add_convert_fusion = bf16[96,4608]{1,0:T(8,128)(2,1)} fusion(bf16[96,4608]{1,0:T(8,128)(2,1)S(1)} %collective-permute-done.3, bf16[4608,192]{0,1:T(8,128)(2,1)S(1)} %copy-done, bf16[192,192]{1,0:T(8,128)(2,1)S(1)} %convolution_convert_fusion.3), kind=kOutput, calls=%fused_computation.5 | convolution fusion | flops 171196416 | bytes 3588096 | tf_op jit(solution)/shard_map/dot_general | solution.py:47
  53.5 0.0 copy-done.4
  53.5 0.0 copy-start.7
  53.5 0.0 copy-start.8
  53.5 0.3 all-to-all-done.1
  53.8 4.9 %all-to-all-start.2 = ((bf16[4,24,4608]{2,1,0:T(8,128)(2,1)}), bf16[4,24,4608]{2,1,0:T(8,128)(2,1)S(1)}, u32[]{:S(2)}, u32[]{:S(2)}) async-start(bf16[4,24,4608]{2,1,0:T(8,128)(2,1)} %bitcast.1), calls=%async_computation.2 | async-start | bytes 1769472 | tf_op jit(solution)/shard_map/all_to_all | solution.py:36
  58.7 1.9 %collective-permute-start.4 = (bf16[96,4608]{1,0:T(8,128)(2,1)S(1)}, bf16[96,4608]{1,0:T(8,128)(2,1)S(1)}, u32[]{:S(2)}, u32[]{:S(2)}) collective-permute-start(bf16[96,4608]{1,0:T(8,128)(2,1)S(1)} %bitcast.17), channel_id=1, source_target_pairs={{0,1},{1,0},{2,3},{3,2},{4,5},{5,4},{6,7},{7,6},{8,9},{9,8},{10,11... | collective-permute-start | bytes 2654216 | tf_op jit(solution)/shard_map/ppermute | solution.py:128
  60.6 0.0 copy-done.7
  60.7 0.0 copy-done.8
  60.7 0.7 convolution_convert_fusion.5
  61.4 1.7 %collective-permute-done.4 = bf16[96,4608]{1,0:T(8,128)(2,1)S(1)} collective-permute-done((bf16[96,4608]{1,0:T(8,128)(2,1)S(1)}, bf16[96,4608]{1,0:T(8,128)(2,1)S(1)}, u32[]{:S(2)}, u32[]{:S(2)}) %collective-permute-start.4) | collective-permute-done | bytes 884768 | tf_op jit(solution)/shard_map/ppermute | solution.py:128
  63.0 0.0 copy-start.1
  63.0 0.7 convolution_convert_fusion.4
  63.7 0.3 fusion.5
  64.1 3.3 %collective-permute-start.5 = (bf16[96,192]{1,0:T(8,128)(2,1)S(1)}, bf16[96,192]{1,0:T(8,128)(2,1)S(1)}, u32[]{:S(2)}, u32[]{:S(2)}) collective-permute-start(bf16[96,192]{1,0:T(8,128)(2,1)S(1)} %slice.129), channel_id=1, source_target_pairs={{0,384},{96,480},{192,576},{288,672},{384,0},{480,96},{576,192},{6... | collective-permute-start | bytes 110600 | tf_op jit(solution)/shard_map/ppermute | solution.py:88
  67.4 4.2 %collective-permute-done.5 = bf16[96,192]{1,0:T(8,128)(2,1)S(1)} collective-permute-done((bf16[96,192]{1,0:T(8,128)(2,1)S(1)}, bf16[96,192]{1,0:T(8,128)(2,1)S(1)}, u32[]{:S(2)}, u32[]{:S(2)}) %collective-permute-start.5) | collective-permute-done | bytes 36896 | tf_op jit(solution)/shard_map/ppermute | solution.py:88
  71.6 0.0 copy-start.2
  71.6 0.6 slice.130
  72.2 0.0 copy-done.1
  72.2 0.0 copy-done.2
  72.2 2.7 %collective-permute-start.6 = (bf16[48,192]{1,0:T(8,128)(2,1)}, bf16[48,192]{1,0:T(8,128)(2,1)}, u32[]{:S(2)}, u32[]{:S(2)}) collective-permute-start(bf16[48,192]{1,0:T(8,128)(2,1)} %slice.130), channel_id=1, source_target_pairs={{0,192},{96,288},{192,0},{288,96},{384,576},{480,672},{576,384},{6... | collective-permute-start | bytes 55304 | tf_op jit(solution)/shard_map/ppermute | solution.py:88
  74.9 0.0 all-to-all-done.2.blocks_ref
  75.0 0.8 shard_map.111
  75.8 8.3 %all-to-all-start.3 = ((bf16[12,2,4608]{2,1,0:T(2,128)(2,1)}), bf16[12,2,4608]{2,1,0:T(2,128)(2,1)S(1)}, u32[]{:S(2)}, u32[]{:S(2)}) async-start(bf16[12,2,4608]{2,1,0:T(2,128)(2,1)} %shard_map.111), calls=%async_computation.3 | async-start | bytes 442368 | tf_op jit(solution)/shard_map/all_to_all | solution.py:36
  84.1 0.0 collective-permute-done.6
  84.1 0.8 slice_add_fusion.1
  84.9 0.0 copy-start.3
  84.9 0.0 copy-start.6
  84.9 6.5 %collective-permute-start.7 = (bf16[24,192]{1,0:T(8,128)(2,1)S(1)}, bf16[24,192]{1,0:T(8,128)(2,1)S(1)}, u32[]{:S(2)}, u32[]{:S(2)}) collective-permute-start(bf16[24,192]{1,0:T(8,128)(2,1)S(1)} %slice.131), channel_id=1, source_target_pairs={{0,96},{96,0},{192,288},{288,192},{384,480},{480,384},{576,672},{6... | collective-permute-start | bytes 27656 | tf_op jit(solution)/shard_map/ppermute | solution.py:88
  91.4 3.3 %convolution_convert_fusion = bf16[4608,192]{0,1:T(8,128)(2,1)} fusion(bf16[96,4608]{1,0:T(8,128)(2,1)} %copy-done.1, bf16[96,4608]{1,0:T(8,128)(2,1)S(1)} %bitcast.19, bf16[192,192]{1,0:T(8,128)(2,1)} %copy-done.4, s32[192]{0:T(256)S(1)} %get-tuple-element.14, s32[192]{0:T(256)S(1)} %broadcast_select_fusion.1), kind=kOutput, calls=%fused_computation | convolution fusion | flops 358391808 | bytes 3614208 | tf_op jit(solution)/shard_map/dot_general | solution.py:47
  94.7 0.0 collective-permute-done.7
  94.7 0.6 fusion.37
  95.3 2.1 %all-to-all-done.3 = bf16[12,2,4608]{2,1,0:T(2,128)(2,1)S(1)} async-done(((bf16[12,2,4608]{2,1,0:T(2,128)(2,1)}), bf16[12,2,4608]{2,1,0:T(2,128)(2,1)S(1)}, u32[]{:S(2)}, u32[]{:S(2)}) %all-to-all-start.3) | async-done | bytes 221216 | tf_op jit(solution)/shard_map/all_to_all | solution.py:36
  97.4 0.0 copy-done.3
  97.4 0.8 fusion.34
  98.1 0.0 copy-done.6
  98.2 0.7 fusion.32
  (8 shorter events, 0.1 us)
Async XLA Ops:
  0.6 46.8 %copy-start = (bf16[4608,192]{0,1:T(8,128)(2,1)S(1)}, bf16[4608,192]{0,1:T(8,128)(2,1)}, u32[]{:S(2)}) copy-start(bf16[4608,192]{0,1:T(8,128)(2,1)} %param.10) | copy-start | bytes 5308420
  2.4 31.2 %all-to-all-start = ((bf16[12,2,4608]{2,1,0:T(2,128)(2,1)}), bf16[12,2,4608]{2,1,0:T(2,128)(2,1)S(1)}, u32[]{:S(2)}, u32[]{:S(2)}) async-start(bf16[12,2,4608]{2,1,0:T(2,128)(2,1)} %broadcast_in_dim.6), calls=%async_computation | async-start | bytes 442368 | tf_op jit(solution)/shard_map/all_to_all | solution.py:36
  17.5 22.1 %copy-start.5 = (bf16[24,192]{1,0:T(8,128)(2,1)S(1)}, bf16[24,192]{1,0:T(8,128)(2,1)}, u32[]{:S(2)}) copy-start(bf16[24,192]{1,0:T(8,128)(2,1)} %param.11) | copy-start | bytes 27652
  17.6 9.7 %collective-permute-start = (bf16[24,192]{1,0:T(8,128)(2,1)}, bf16[24,192]{1,0:T(8,128)(2,1)S(1)}, u32[]{:S(2)}, u32[]{:S(2)}) collective-permute-start(bf16[24,192]{1,0:T(8,128)(2,1)} %param.11), channel_id=1, source_target_pairs={{0,96},{96,0},{192,288},{288,192},{384,480},{480,384},{576,672},{6... | collective-permute-start | bytes 27656 | tf_op jit(solution)/shard_map/ppermute | solution.py:81
  28.0 11.7 %collective-permute-start.1 = (bf16[48,192]{1,0:T(8,128)(2,1)S(1)}, bf16[48,192]{1,0:T(8,128)(2,1)S(1)}, u32[]{:S(2)}, u32[]{:S(2)}) collective-permute-start(bf16[48,192]{1,0:T(8,128)(2,1)S(1)} %pad_maximum_fusion.1), channel_id=1, source_target_pairs={{0,192},{96,288},{192,0},{288,96},{384,576},{480,672},{576,384},{6... | collective-permute-start | bytes 55304 | tf_op jit(solution)/shard_map/ppermute | solution.py:81
  34.6 19.2 %all-to-all-start.1 = ((bf16[4,24,4608]{2,1,0:T(8,128)(2,1)}), bf16[4,24,4608]{2,1,0:T(8,128)(2,1)S(1)}, u32[]{:S(2)}, u32[]{:S(2)}) async-start(bf16[4,24,4608]{2,1,0:T(8,128)(2,1)} %broadcast_in_dim.8), calls=%async_computation.1 | async-start | bytes 1769472 | tf_op jit(solution)/shard_map/all_to_all | solution.py:36
  39.7 7.5 %collective-permute-start.2 = (bf16[96,192]{1,0:T(8,128)(2,1)S(1)}, bf16[96,192]{1,0:T(8,128)(2,1)S(1)}, u32[]{:S(2)}, u32[]{:S(2)}) collective-permute-start(bf16[96,192]{1,0:T(8,128)(2,1)S(1)} %pad_maximum_fusion), channel_id=1, source_target_pairs={{0,384},{96,480},{192,576},{288,672},{384,0},{480,96},{576,192},{6... | collective-permute-start | bytes 110600 | tf_op jit(solution)/shard_map/ppermute | solution.py:81
  47.2 6.3 %copy-start.4 = (bf16[192,192]{1,0:T(8,128)(2,1)}, bf16[192,192]{1,0:T(8,128)(2,1)S(1)}, u32[]{:S(2)}) copy-start(bf16[192,192]{1,0:T(8,128)(2,1)S(1)} %constant_dynamic-update-slice_fusion) | copy-start | bytes 221188
  47.8 4.3 %collective-permute-start.3 = (bf16[96,4608]{1,0:T(8,128)(2,1)S(1)}, bf16[96,4608]{1,0:T(8,128)(2,1)S(1)}, u32[]{:S(2)}, u32[]{:S(2)}) collective-permute-start(bf16[96,4608]{1,0:T(8,128)(2,1)S(1)} %convolution_convert_fusion.1), channel_id=1, source_target_pairs={{0,1},{1,0},{2,3},{3,2},{4,5},{5,4},{6,7},{7,6},{8,9},{9,8},{10,11... | collective-permute-start | bytes 2654216 | tf_op jit(solution)/shard_map/ppermute | solution.py:121
  53.5 7.2 %copy-start.7 = (s32[192]{0:T(256)S(1)}, s32[192]{0:T(256)}, u32[]{:S(2)}) copy-start(s32[192]{0:T(256)} %constant.57.clone) | copy-start | bytes 2308
  53.5 7.2 %copy-start.8 = (s32[192]{0:T(256)S(1)}, s32[192]{0:T(256)}, u32[]{:S(2)}) copy-start(s32[192]{0:T(256)} %constant.56.clone) | copy-start | bytes 2308
  53.8 21.2 %all-to-all-start.2 = ((bf16[4,24,4608]{2,1,0:T(8,128)(2,1)}), bf16[4,24,4608]{2,1,0:T(8,128)(2,1)S(1)}, u32[]{:S(2)}, u32[]{:S(2)}) async-start(bf16[4,24,4608]{2,1,0:T(8,128)(2,1)} %bitcast.1), calls=%async_computation.2 | async-start | bytes 1769472 | tf_op jit(solution)/shard_map/all_to_all | solution.py:36
  58.7 4.3 %collective-permute-start.4 = (bf16[96,4608]{1,0:T(8,128)(2,1)S(1)}, bf16[96,4608]{1,0:T(8,128)(2,1)S(1)}, u32[]{:S(2)}, u32[]{:S(2)}) collective-permute-start(bf16[96,4608]{1,0:T(8,128)(2,1)S(1)} %bitcast.17), channel_id=1, source_target_pairs={{0,1},{1,0},{2,3},{3,2},{4,5},{5,4},{6,7},{7,6},{8,9},{9,8},{10,11... | collective-permute-start | bytes 2654216 | tf_op jit(solution)/shard_map/ppermute | solution.py:128
  63.0 9.2 %copy-start.1 = (bf16[96,4608]{1,0:T(8,128)(2,1)}, bf16[96,4608]{1,0:T(8,128)(2,1)S(1)}, u32[]{:S(2)}) copy-start(bf16[96,4608]{1,0:T(8,128)(2,1)S(1)} %collective-permute-done.4) | copy-start | bytes 2654212
  64.1 7.5 %collective-permute-start.5 = (bf16[96,192]{1,0:T(8,128)(2,1)S(1)}, bf16[96,192]{1,0:T(8,128)(2,1)S(1)}, u32[]{:S(2)}, u32[]{:S(2)}) collective-permute-start(bf16[96,192]{1,0:T(8,128)(2,1)S(1)} %slice.129), channel_id=1, source_target_pairs={{0,384},{96,480},{192,576},{288,672},{384,0},{480,96},{576,192},{6... | collective-permute-start | bytes 110600 | tf_op jit(solution)/shard_map/ppermute | solution.py:88
  71.6 0.6 copy-start.2
  72.2 11.8 %collective-permute-start.6 = (bf16[48,192]{1,0:T(8,128)(2,1)}, bf16[48,192]{1,0:T(8,128)(2,1)}, u32[]{:S(2)}, u32[]{:S(2)}) collective-permute-start(bf16[48,192]{1,0:T(8,128)(2,1)} %slice.130), channel_id=1, source_target_pairs={{0,192},{96,288},{192,0},{288,96},{384,576},{480,672},{576,384},{6... | collective-permute-start | bytes 55304 | tf_op jit(solution)/shard_map/ppermute | solution.py:88
  75.8 21.6 %all-to-all-start.3 = ((bf16[12,2,4608]{2,1,0:T(2,128)(2,1)}), bf16[12,2,4608]{2,1,0:T(2,128)(2,1)S(1)}, u32[]{:S(2)}, u32[]{:S(2)}) async-start(bf16[12,2,4608]{2,1,0:T(2,128)(2,1)} %shard_map.111), calls=%async_computation.3 | async-start | bytes 442368 | tf_op jit(solution)/shard_map/all_to_all | solution.py:36
  84.9 12.5 %copy-start.3 = (bf16[2,4608]{1,0:T(2,128)(2,1)S(1)}, bf16[2,4608]{1,0:T(2,128)(2,1)}, u32[]{:S(2)}) copy-start(bf16[2,4608]{1,0:T(2,128)(2,1)} %param.8) | copy-start | bytes 55300
  84.9 13.3 %copy-start.6 = (bf16[2,4608]{1,0:T(2,128)(2,1)S(1)}, bf16[2,4608]{1,0:T(2,128)(2,1)}, u32[]{:S(2)}) copy-start(bf16[2,4608]{1,0:T(2,128)(2,1)} %param.9) | copy-start | bytes 55300
  84.9 9.8 %collective-permute-start.7 = (bf16[24,192]{1,0:T(8,128)(2,1)S(1)}, bf16[24,192]{1,0:T(8,128)(2,1)S(1)}, u32[]{:S(2)}, u32[]{:S(2)}) collective-permute-start(bf16[24,192]{1,0:T(8,128)(2,1)S(1)} %slice.131), channel_id=1, source_target_pairs={{0,96},{96,0},{192,288},{288,192},{384,480},{480,384},{576,672},{6... | collective-permute-start | bytes 27656 | tf_op jit(solution)/shard_map/ppermute | solution.py:88
